TPU v7x, 512 devices: a whole 4x8x8 slice. The times are simulated.
512 devices in a mesh: users: 64 (over y, z_hi, x), cand: 8 (over z_lo, core).
Axes of the slice: x: 4, y: 8, z: 8 (z_hi: 2, z_lo: 4; z = z_hi * 4 + z_lo), core: 2. Of those that a mesh axis runs over, the one named last changes fastest.
Arguments:
- candidate_rows: bfloat16 [32768, 1024], P(('users', 'cand')), may hold values from -6 to 6
- weight_in: bfloat16 [2, 1024, 8, 512], P(None, None, 'cand'), may hold values from -0.1875 to 0.1875
- weight_out: bfloat16 [2, 8, 128, 1024], P(None, 'cand'), may hold values from -0.1875 to 0.1875
- history_cache: bfloat16 [2, 2, 8192, 8, 128], P(None, None, 'users', 'cand'), may hold values from -6 to 6
- block_user: int32 [64], replicated, may hold values from 0 to 15, as said below
- block_offset: int32 [64], replicated, may hold values from 0 to 31, as said below
- history_length: int32 [16], replicated, may hold values from 1 to 4096, as said below
- candidate_count: int32 [16], replicated, may hold values from 1 to 16384, as said below
Outputs:
- scored_rows: bfloat16 [32768, 1024], P(('users', 'cand'))
Inputs may be any that keep to these rules, and one draw needn't show every extreme that they name: `block_user`: every one of the 16 users owns at least one block; the blocks of one user may stand anywhere; exactly one user owns 64 / 2 blocks, every other user fewer. `block_offset`: the blocks of a user that owns b blocks carry the offsets 0 to b - 1, each once. `history_length`: a user that owns b blocks has more than (b - 1) * 128 and at most b * 128 history rows. `candidate_count`: the counts sum to 32768; the rows of one user are consecutive, users in increasing order.
All inputs are finite; a program needn't handle non-finite values.
Results may differ from a plain program's by a relative error of at most 0.027.
Values may be sent and summed in bfloat16 or wider, within the bound.
A program may use at most 64 MiB of HBM per device.

v0:
```python
import math

import jax
import jax.numpy as jnp
from jax import lax
from jax.sharding import PartitionSpec as P

BLOCK = 128


def body(
    candidate_rows,
    weight_in,
    weight_out,
    history_cache,
    block_user,
    block_offset,
    history_length,
    candidate_count,
):
    own_rows, model_width = candidate_rows.shape
    layers, model_again, heads_here, packed = weight_in.shape
    head_dim = packed // 4
    cand_devices = lax.axis_size("cand")
    row_count = own_rows * cand_devices
    score_scale = 1.0 / math.sqrt(head_dim)
    user_count = history_length.shape[0]
    users_all = jnp.arange(user_count, dtype=jnp.int32)
    user_ends = jnp.cumsum(candidate_count)
    group_rows = lax.axis_index("users") * row_count + jnp.arange(row_count, dtype=jnp.int32)
    cand_user = jnp.sum((group_rows[:, None] >= user_ends[None, :]).astype(jnp.int32), axis=1)
    step_rows = 4 * BLOCK

    def block_term(accumulated, key_value, piece_start, queries):
        span_rows = key_value.shape[1]
        span_blocks = span_rows // BLOCK
        first_block = piece_start // BLOCK
        owners = lax.dynamic_slice_in_dim(block_user, first_block, span_blocks)
        places = lax.dynamic_slice_in_dim(block_offset, first_block, span_blocks)
        row_user = jnp.broadcast_to(owners[:, None], (span_blocks, BLOCK)).reshape(span_rows)
        row_place = (places[:, None] * BLOCK + jnp.arange(BLOCK, dtype=jnp.int32)[None, :]).reshape(
            span_rows
        )
        row_length = jnp.sum(
            jnp.where(row_user[:, None] == users_all[None, :], history_length[None, :], 0), axis=1
        )
        visible = (cand_user[:, None] == row_user[None, :]) & (row_place < row_length)[None, :]
        scores = (
            jnp.einsum("rhd,nhd->hrn", queries, key_value[0], preferred_element_type=jnp.float32)
            * score_scale
        )
        weights = jnp.where(visible[None], jax.nn.silu(scores), 0.0).astype(jnp.bfloat16)
        return accumulated + jnp.einsum(
            "hrn,nhd->rhd", weights, key_value[1], preferred_element_type=jnp.float32
        )

    current_own = candidate_rows
    for layer_index in range(layers):
        project_segment = lax.all_gather(current_own, "cand", axis=0, tiled=True)
        flat = weight_in[layer_index].reshape(model_width, heads_here * packed)
        mixed = jnp.dot(project_segment, flat, preferred_element_type=jnp.float32)
        projected = (
            jax.nn.silu(mixed)
            .astype(jnp.bfloat16)
            .reshape(project_segment.shape[0], heads_here, 4, head_dim)
        )
        gate_part = projected[:, :, 0]
        values_part = projected[:, :, 1]
        queries = projected[:, :, 2]
        keys_part = projected[:, :, 3]
        own_score = (
            jnp.sum(queries.astype(jnp.float32) * keys_part.astype(jnp.float32), axis=-1)
            * score_scale
        )
        own_weight = jax.nn.silu(own_score).astype(jnp.bfloat16)
        own_term = own_weight.astype(jnp.float32)[..., None] * values_part.astype(jnp.float32)
        empty_sum = jnp.zeros((row_count, heads_here, head_dim), jnp.float32)
        segment = lax.all_gather(history_cache[layer_index], "users", axis=1, tiled=True)
        fold_span_rows = segment.shape[1]
        turns = fold_span_rows // step_rows

        def advance(position, running):
            sliced = lax.dynamic_slice_in_dim(segment, position * step_rows, step_rows, 1)
            return block_term(running, sliced, position * step_rows, queries)

        attended = lax.fori_loop(0, turns, advance, empty_sum)
        attended = attended + own_term
        centred = attended - jnp.mean(attended, axis=-1, keepdims=True)
        variance = jnp.mean(centred * centred, axis=-1, keepdims=True)
        gated = (centred * lax.rsqrt(variance + 1e-05) * gate_part.astype(jnp.float32)).astype(
            jnp.bfloat16
        )
        partial_out = jnp.dot(
            gated.reshape(row_count, heads_here * head_dim),
            weight_out[layer_index].reshape(heads_here * head_dim, model_width),
            preferred_element_type=jnp.float32,
        )
        shared = lax.psum_scatter(
            partial_out.astype(jnp.bfloat16), "cand", scatter_dimension=0, tiled=True
        ).astype(jnp.float32)
        current_own = (current_own.astype(jnp.float32) + shared).astype(jnp.bfloat16)
    return current_own


def solution(mesh):
    placed = (
        P(("users", "cand"), None),
        P(None, None, "cand", None),
        P(None, "cand", None, None),
        P(None, None, "users", "cand", None),
        P(),
        P(),
        P(),
        P(),
    )
    return jax.shard_map(
        body, mesh=mesh, in_specs=placed, out_specs=P(("users", "cand"), None), check_vma=False
    )
```

profile of v0, /device:TPU:1, one launch (start us, length us, event | category | flops | bytes accessed | tf_op | source)
XLA Modules:
  0.0 568.4 jit_solution(17218734392977073218)
XLA Ops:
  6.5 0.7 all-gather.7.cloned.1.call-update
  7.3 1.5 fusion.74
  8.9 0.7 copy.22
  9.7 0.1 reduce.6
  9.9 42.9 %all-gather.7.cloned.1.call-done = bf16[512,1024]{1,0:T(8,128)(2,1)} async-done(((bf16[64,1024]{1,0:T(8,128)(2,1)}), bf16[512,1024]{1,0:T(8,128)(2,1)}) %all-gather.7.cloned.1.call-update) | async-done | bytes 1048592 | tf_op jit(solution)/shard_map/all_gather | solution.py:59
  52.8 2.4 multiply_convert_fusion.1
  55.3 0.1 copy.24
  55.5 157.6 %all-gather.11.cloned.1.call-done = bf16[1,2,8192,1,128]{4,2,1,3,0:T(8,128)(2,1)} async-done(((bf16[1,2,128,1,128]{4,2,1,3,0:T(8,128)(2,1)}), bf16[1,2,8192,1,128]{4,2,1,3,0:T(8,128)(2,1)}) %all-gather.11.cloned.1.call-update) | async-done | bytes 4194320 | tf_op jit(solution)/shard_map/all_gather | solution.py:78
  213.1 35.4 %while.32 = (s32[]{:T(128)}, f32[512,1,128]{0,2,1:T(8,128)S(1)}, bf16[2,8192,1,128]{3,1,2,0:T(8,128)(2,1)}, s32[512]{0:T(512)S(1)}, s32[64]{0:T(128)S(1)}, /*ind...) while((s32[]{:T(128)}, f32[512,1,128]{0,2,1:T(8,128)S(1)}, ...), condition=%wide.region_4.5_spmd.clone, body=%wide.region_2.4_spmd.clone.sunk | while | flops 136733216 | bytes 933431 | solution.py:86
  213.3 0.1 select_reduce_fusion.4
  213.6 1.8 fusion.82
  215.5 0.1 select_reduce_fusion.4
  215.8 1.8 fusion.82
  217.7 0.1 select_reduce_fusion.4
  218.0 1.8 fusion.82
  219.9 0.1 select_reduce_fusion.4
  220.2 1.8 fusion.82
  222.1 0.1 select_reduce_fusion.4
  222.4 1.8 fusion.82
  224.4 0.1 select_reduce_fusion.4
  224.6 1.8 fusion.82
  226.6 0.1 select_reduce_fusion.4
  226.8 1.8 fusion.82
  228.8 0.1 select_reduce_fusion.4
  229.0 1.8 fusion.82
  231.0 0.1 select_reduce_fusion.4
  231.2 1.8 fusion.82
  233.2 0.1 select_reduce_fusion.4
  233.4 1.8 fusion.82
  235.4 0.1 select_reduce_fusion.4
  235.7 1.8 fusion.82
  237.9 1.8 fusion.82
  240.1 1.8 fusion.82
  242.3 1.8 fusion.82
  244.5 1.8 fusion.82
  246.7 1.8 fusion.82
  248.7 1.5 convolution_convert_fusion.1
  250.2 35.8 %reduce-scatter.3.cloned.1.call-done = bf16[64,1024]{1,0:T(8,128)(2,1)} async-done(((bf16[512,1024]{1,0:T(8,128)(2,1)}), bf16[64,1024]{1,0:T(8,128)(2,1)}) %reduce-scatter.3.cloned.1.call-update) | async-done | bytes 131088 | tf_op jit(solution)/shard_map/reduce_scatter | solution.py:98
  286.0 1.6 add_convert_fusion.1
  287.7 0.5 all-gather.13.cloned.1.call-update
  288.3 38.3 %all-gather.9.cloned.1.call-done = bf16[512,1024]{1,0:T(8,128)(2,1)} async-done(((bf16[64,1024]{1,0:T(8,128)(2,1)}), bf16[512,1024]{1,0:T(8,128)(2,1)}) %all-gather.9.cloned.1.call-update) | async-done | bytes 1048592 | tf_op jit(solution)/shard_map/all_gather | solution.py:59
  326.6 2.4 multiply_convert_fusion
  329.1 0.1 copy.27
  329.3 157.7 %all-gather.13.cloned.1.call-done = bf16[1,2,8192,1,128]{4,2,1,3,0:T(8,128)(2,1)} async-done(((bf16[1,2,128,1,128]{4,2,1,3,0:T(8,128)(2,1)}), bf16[1,2,8192,1,128]{4,2,1,3,0:T(8,128)(2,1)}) %all-gather.13.cloned.1.call-update) | async-done | bytes 4194320 | tf_op jit(solution)/shard_map/all_gather | solution.py:78
  487.0 35.3 %while.33 = (s32[]{:T(128)}, f32[512,1,128]{0,2,1:T(8,128)S(1)}, bf16[2,8192,1,128]{3,1,2,0:T(8,128)(2,1)}, s32[512]{0:T(512)S(1)}, s32[64]{0:T(128)S(1)}, /*ind...) while((s32[]{:T(128)}, f32[512,1,128]{0,2,1:T(8,128)S(1)}, ...), condition=%wide.region_11.12_spmd.clone, body=%wide.region_9.11_spmd.clone.sunk | while | flops 136733216 | bytes 933431 | solution.py:86
  487.4 1.8 fusion.84
  489.6 1.8 fusion.84
  491.8 1.8 fusion.84
  494.0 1.8 fusion.84
  496.2 1.8 fusion.84
  498.4 1.8 fusion.84
  500.6 1.8 fusion.84
  502.9 1.8 fusion.84
  505.1 1.8 fusion.84
  507.3 1.8 fusion.84
  509.5 1.8 fusion.84
  511.7 1.8 fusion.84
  513.9 1.8 fusion.84
  516.1 1.8 fusion.84
  518.3 1.8 fusion.84
  520.5 1.8 fusion.84
  522.5 1.5 convolution_convert_fusion
  524.0 35.9 %reduce-scatter.5.cloned.1.call-done = bf16[64,1024]{1,0:T(8,128)(2,1)} async-done(((bf16[512,1024]{1,0:T(8,128)(2,1)}), bf16[64,1024]{1,0:T(8,128)(2,1)}) %reduce-scatter.5.cloned.1.call-update) | async-done | bytes 131088 | tf_op jit(solution)/shard_map/reduce_scatter | solution.py:98
  559.9 1.6 add_convert_fusion
  (190 shorter events, 12.4 us)
Async XLA Ops:
  6.5 46.3 %all-gather.7.cloned.1.call-start = ((), (), s32[]{:S(2)}) async-start(), calls=%async_computation.2 | async-start | bytes 1179648 | tf_op jit(solution)/shard_map/all_gather | solution.py:59
  7.3 205.8 %all-gather.11.cloned.1.call-start = ((), (), s32[]{:S(2)}) async-start(), calls=%async_computation.6 | async-start | bytes 4259840 | tf_op jit(solution)/shard_map/all_gather | solution.py:78
  8.9 277.2 %reduce-scatter.3.cloned.1.call-start = ((), (), s32[]{:S(2)}) async-start(), calls=%async_computation.3 | async-start | bytes 1179648 | tf_op jit(solution)/shard_map/reduce_scatter | solution.py:98
  9.9 203.2 %copy-start.3 = (s32[16]{0:T(128)S(1)}, s32[16]{0:T(128)}, u32[]{:S(2)}) copy-start(s32[16]{0:T(128)} %param.18) | copy-start | bytes 196
  9.9 203.2 %copy-start.4 = (s32[64]{0:T(128)S(1)}, s32[64]{0:T(128)}, u32[]{:S(2)}) copy-start(s32[64]{0:T(128)} %param.16) | copy-start | bytes 772
  9.9 203.2 %copy-start.5 = (s32[64]{0:T(128)S(1)}, s32[64]{0:T(128)}, u32[]{:S(2)}) copy-start(s32[64]{0:T(128)} %param.17) | copy-start | bytes 772
  213.1 35.6 %copy-start.2 = (bf16[2,1,128,1024]{3,2,1,0:T(8,128)(2,1)S(1)}, bf16[2,1,128,1024]{3,2,1,0:T(8,128)(2,1)}, u32[]{:S(2)}) copy-start(bf16[2,1,128,1024]{3,2,1,0:T(8,128)(2,1)} %param.14) | copy-start | bytes 1572868
  213.1 72.9 %copy-start.1 = (bf16[64,1024]{1,0:T(8,128)(2,1)S(1)}, bf16[64,1024]{1,0:T(8,128)(2,1)}, u32[]{:S(2)}) copy-start(bf16[64,1024]{1,0:T(8,128)(2,1)} %param.12) | copy-start | bytes 393220
  250.1 76.5 %all-gather.9.cloned.1.call-start = ((), (), s32[]{:S(2)}) async-start(), calls=%async_computation.4 | async-start | bytes 1179648 | tf_op jit(solution)/shard_map/all_gather | solution.py:59
  287.7 199.3 %all-gather.13.cloned.1.call-start = ((), (), s32[]{:S(2)}) async-start(), calls=%async_computation.7 | async-start | bytes 4259840 | tf_op jit(solution)/shard_map/all_gather | solution.py:78
  288.2 271.7 %reduce-scatter.5.cloned.1.call-start = ((), (), s32[]{:S(2)}) async-start(), calls=%async_computation.5 | async-start | bytes 1179648 | tf_op jit(solution)/shard_map/reduce_scatter | solution.py:98
  487.0 72.9 %copy-start = (bf16[64,1024]{1,0:T(8,128)(2,1)S(1)}, bf16[64,1024]{1,0:T(8,128)(2,1)}, u32[]{:S(2)}) copy-start(bf16[64,1024]{1,0:T(8,128)(2,1)} %add_convert_fusion.1) | copy-start | bytes 393220
Sparse Core Ops, SparseCore 0:
  9.4 43.3 all-gather.6
  57.2 155.8 all-gather.10
  250.3 35.7 reduce-scatter.2
  288.0 38.6 all-gather.8
  330.9 156.0 all-gather.12
  524.1 35.7 reduce-scatter.4
where the time goes:
time: 571 us; the launch traced here: 568 us
  waiting for transfers between devices  470 us (82%)
  matrix products  64.3 us (11%)
  between operations  13.6 us (2%)
  other arithmetic  11.6 us (2%)
  local copies, waits for them, and re-layouts  7.34 us (1%)
    all_gather x2, waiting for transfers between devices, body(): lax.all_gather(history_cache[layer_index], 'users', axis=1, tiled=True)  315 us
    all_gather x2, waiting for transfers between devices, body(): project_segment = lax.all_gather(current_own, 'cand', axis=0, tiled=True)  81.2 us
    reduce_scatter x2, waiting for transfers between devices, body(): lax.psum_scatter(partial_out.astype(jnp.bfloat16), 'cand', scatter_dimens...  71.7 us
    dot_general x32, matrix products, block_term(): jnp.einsum('hrn,nhd->rhd', weights, key_value[1], preferred_element_type=...  56.5 us
  transfers between devices with their start and end apart: 6, of which 6 were waited for; matrix products, arithmetic and copies ran while one was open for 1% of the time, Pallas kernels for 0%

commit v1 on v0

v1 whole, which is shorter than its diff:
```python
import math

import jax
import jax.numpy as jnp
from jax import lax
from jax.experimental import pallas as pl
from jax.experimental.pallas import tpu as pltpu
from jax.sharding import PartitionSpec as P

BLOCK = 128
NX, NY, NZ, NC = 4, 8, 2, 8
ROWS_A, ROWS_B = 48, 80
OWN, D, DH, USERS = 64, 1024, 128, 16
GROUP = OWN * NC
HIDE = -1e30
CHUNKS = 2
MESSAGES = 200
SCALE = 1.0 / math.sqrt(DH)


def half_silu(h):
    return h * jnp.tanh(h) + h


def kernel(
    x_ref, win_ref, wout_ref, hist_ref, user_ref, place_ref, length_ref, count_ref, out_ref,
    kva, kvb, ma, mb, xg, x1, win, wout, qp, gate, acc, gat, gown, g1,
    send_sem, recv_sem, local_sem,
):
    u, c = lax.axis_index("users"), lax.axis_index("cand")
    y, zh, x = u // 8, (u // 4) % 2, u % 4
    zl, core = c // 2, c % 2
    sib = zl * 2 + (1 - core)

    def at(y_, zh_, x_):
        return y_ * 8 + zh_ * 4 + x_

    xs = [(x + k) % NX for k in range(NX)]
    ys = [(y + k) % NY for k in range(NY)]
    right, left = (at(y, zh, xs[1]), c), (at(y, zh, xs[3]), c)
    up, down = (at(ys[1], zh, x), c), (at(ys[7], zh, x), c)
    over = (at(y, 1 - zh, x), c)
    z8 = zh * 4 + zl
    zu, zd = (z8 + 1) % 8, (z8 + 7) % 8
    ring_up = (at(y, zu // 4, x), (zu % 4) * 2 + core)
    ring_down = (at(y, zd // 4, x), (zd % 4) * 2 + core)
    zls = [(zl + k) % 4 for k in range(4)]

    def line(k):
        return (u, zls[k] * 2 + core)

    local = []

    def fetch(src, dst):
        copy = pltpu.make_async_copy(src, dst, local_sem.at[len(local)])
        copy.start()
        local.append(copy)
        return copy

    first = [fetch(x_ref, xg.at[c])]
    for l in range(2):
        first.append(fetch(hist_ref.at[l, :, pl.ds(0, ROWS_A)], kva.at[l, zh, y, x]))
        first.append(fetch(hist_ref.at[l, :, pl.ds(ROWS_A, ROWS_B)], kvb.at[l, zh, x, y]))
    second = [fetch(wout_ref.at[l], wout.at[l, c]) for l in range(2)]
    third = [fetch(win_ref.at[l], win.at[l]) for l in range(2)]

    barrier = pltpu.get_barrier_semaphore()
    friends = [right, left, up, down, over, ring_up, ring_down]
    friends += [(u, (c + k) % NC) for k in range(1, NC)]
    for friend in friends:
        pl.semaphore_signal(barrier, inc=1, device_id=friend, device_id_type=pl.DeviceIdType.MESH)
    pl.semaphore_wait(barrier, len(friends))

    sent = []

    def send(src, dst, to):
        n = len(sent)
        copy = pltpu.make_async_remote_copy(
            src_ref=src, dst_ref=dst, send_sem=send_sem.at[n], recv_sem=recv_sem.at[n],
            device_id=to, device_id_type=pl.DeviceIdType.MESH,
        )
        copy.start()
        sent.append(copy)
        return copy

    def same(ref, to):
        return send(ref, ref, to)

    def got(copies):
        for copy in copies:
            copy.wait_recv()

    class Chain:
        def __init__(self, l, z):
            self.l, self.z = l, z

        def a(self, yy, *rest):
            return kva.at[(self.l, self.z, yy) + rest]

        def b(self, xx, *rest):
            return kvb.at[(self.l, self.z, xx) + rest]

        def r0(self):
            s = self.a(y, x)
            self.ax = [same(s, right), same(s, left)]
            s = self.b(x, y)
            self.by = [same(s, up), same(s, down)]

        def r1(self):
            got(self.ax)
            self.ax = [same(self.a(y, xs[3], 0), right), same(self.a(y, xs[1], 1), left)]
            got(self.by)
            self.by = [same(self.b(x, ys[7]), up), same(self.b(x, ys[1]), down)]

        def r2(self):
            got(self.ax)
            s = self.a(y)
            self.ay = [same(s, up), same(s, down)]
            got(self.by)
            self.by = [same(self.b(x, ys[6]), up), same(self.b(x, ys[2]), down)]

        def r3(self):
            got(self.by)
            self.by = [same(self.b(x, ys[5], 0), up), same(self.b(x, ys[3], 1), down)]
            got(self.ay)
            self.ay = [same(self.a(ys[7]), up), same(self.a(ys[1]), down)]

        def r4(self):
            got(self.by)
            s = self.b(x)
            self.bx = [same(s, right), same(s, left)]
            got(self.ay)
            self.ay = [same(self.a(ys[6]), up), same(self.a(ys[2]), down)]

        def r5(self):
            got(self.ay)
            self.ay = [
                same(self.a(ys[5], pl.ds(0, 2)), up),
                same(self.a(ys[3], pl.ds(2, 2)), down),
            ]

        def r6(self):
            got(self.ay)

        def r7(self):
            got(self.bx)
            self.bx = [
                same(self.b(xs[3], pl.ds(0, 4)), right),
                same(self.b(xs[1], pl.ds(4, 4)), left),
            ]

        def r8(self):
            got(self.bx)

    def scores(rows, k, m, v):
        s = lax.dot_general(
            qp[rows, :], jnp.concatenate([k, m], axis=1), (((1,), (1,)), ((), ())),
            preferred_element_type=jnp.float32,
        )
        w = half_silu(jnp.maximum(s * (0.5 * SCALE), -100.0)).astype(jnp.bfloat16)
        acc[rows, :] += jnp.dot(w, v, preferred_element_type=jnp.float32)

    def attend_a(l, offsets):
        low, step = offsets[0], (offsets[1] - offsets[0]) if len(offsets) > 1 else 1

        @pl.loop(0, 2 * len(offsets))
        def _(i):
            yy = (y + low + (i // 2) * step) % NY
            rows = pl.ds(pl.multiple_of((i % 2) * 256, 256), 256)
            n = NZ * NX * ROWS_A
            scores(
                rows,
                kva[l, :, yy, :, 0].reshape(n, DH),
                ma[:, yy].reshape(n, DH),
                kva[l, :, yy, :, 1].reshape(n, DH),
            )

    def attend_b(l, chunks):
        where, number = chunks

        @pl.loop(0, 2 * number)
        def _(i):
            zz, xx = where(i // 2)
            rows = pl.ds(pl.multiple_of((i % 2) * 256, 256), 256)
            n = NY * ROWS_B
            scores(
                rows,
                kvb[l, zz, xx, :, 0].reshape(n, DH),
                mb[zz, xx].reshape(n, DH),
                kvb[l, zz, xx, :, 1].reshape(n, DH),
            )

    def project(l, rows, value):
        mixed = jnp.dot(value, win[l], preferred_element_type=jnp.float32)
        p = half_silu(0.5 * mixed).astype(jnp.bfloat16)
        q = p[:, 2 * DH:3 * DH]
        gate[rows, :] = p[:, :DH]
        qp[rows, pl.ds(0, DH)] = q
        own = jnp.sum(
            q.astype(jnp.float32) * p[:, 3 * DH:].astype(jnp.float32), axis=1, keepdims=True
        )
        own = half_silu(own * (0.5 * SCALE)).astype(jnp.bfloat16).astype(jnp.float32)
        acc[rows, :] = own * p[:, DH:2 * DH].astype(jnp.float32)

    def gated(rows):
        a = acc[rows, :]
        centred = a - jnp.mean(a, axis=1, keepdims=True)
        variance = jnp.mean(centred * centred, axis=1, keepdims=True)
        return (
            centred * lax.rsqrt(variance + 1e-05) * gate[rows, :].astype(jnp.float32)
        ).astype(jnp.bfloat16)

    class Weights:
        def __init__(self, l):
            self.l = l

        def slot(self, k):
            return zls[k % 4] * 2 + core

        def w1(self):
            s = wout.at[self.l, c]
            self.z = [same(s, ring_up), same(s, ring_down)]
            self.s = [same(s, (u, sib))]

        def w2(self):
            got(self.z)
            below, above = wout.at[self.l, self.slot(3)], wout.at[self.l, self.slot(1)]
            self.z = [
                same(below.at[pl.ds(0, 64)], ring_up), same(above.at[pl.ds(64, 64)], ring_down)
            ]
            self.s += [same(below, (u, sib)), same(above, (u, sib))]

        def w3(self):
            got(self.z)
            self.s += [same(wout.at[self.l, self.slot(2)], (u, sib))]

        def w4(self):
            got(self.s)

    for copy in first:
        copy.wait()
    xsend = [same(xg.at[c], line(k)) for k in range(1, 4)]
    xshare = [same(xg.at[c], (u, sib))]
    across = []
    for l in range(2):
        across.append([same(kva.at[l, zh, y, x], over), same(kvb.at[l, zh, x, y], over)])
        if l == 0:
            chains = [[Chain(i, zh), Chain(i, 1 - zh)] for i in range(2)]
            o, p = chains[0]
            o.r0()
    o1, p1 = chains[1]
    w0, w1 = Weights(0), Weights(1)

    lane = lax.broadcasted_iota(jnp.int32, (BLOCK, BLOCK), 1)
    sub = lax.broadcasted_iota(jnp.int32, (BLOCK, BLOCK), 0)

    @pl.loop(0, NX * NY * NZ)
    def _(b):
        by, bz, bx = b // 8, (b // 4) % 2, b % 4
        owner = user_ref[b]
        valid = length_ref[owner] - place_ref[b] * BLOCK
        code = jnp.where(sub < valid, owner, USERS)
        hot = jnp.where(lane == code, 1.0, 0.0).astype(jnp.bfloat16)
        ma[bz, by, bx] = hot[:ROWS_A]
        mb[bz, bx, by] = hot[ROWS_A:]

    o.r1()

    @pl.loop(0, GROUP // BLOCK)
    def _(t):
        row = u * GROUP + t * BLOCK + sub
        end = count_ref[0]
        cu = (row >= end).astype(jnp.int32)
        for k in range(1, USERS):
            end = end + count_ref[k]
            cu = cu + (row >= end).astype(jnp.int32)
        hide = jnp.where((lane == cu) | (lane > USERS), 0.0, HIDE)
        qp[pl.ds(pl.multiple_of(t * BLOCK, BLOCK), BLOCK), pl.ds(DH, DH)] = hide.astype(jnp.bfloat16)

    got(across[0])
    p.r0()
    o.r2()
    p.r1()
    o.r3()
    for k in range(1, 4):
        got([xsend[k - 1]])
        xshare.append(same(xg.at[zls[4 - k] * 2 + core], (u, sib)))
    for copy in second:
        copy.wait()
    w0.w1()
    p.r2()
    o.r4()
    for copy in third:
        copy.wait()
    got(xshare)

    @pl.loop(0, 4)
    def _(t):
        part = pl.ds(pl.multiple_of(t * 2, 2), 2)
        rows = pl.ds(pl.multiple_of(t * BLOCK, BLOCK), BLOCK)
        project(0, rows, xg[part].reshape(BLOCK, D))

    p.r3()
    w0.w2()
    o.r5()
    p.r4()
    attend_a(0, [-1 + NY, NY, NY + 1])
    got(across[1])
    o1.r0()
    p1.r0()
    w0.w3()
    p.r5()
    o.r6()
    attend_a(0, [2, 6])
    o1.r1()
    p1.r1()
    p.r6()
    attend_b(0, (lambda i: (i, x), 2))
    o.r7()
    o1.r2()
    p1.r2()
    attend_a(0, [3, 4, 5])
    attend_b(0, (lambda i: (zh, (x + 1 + 2 * i) % NX), 2))
    p.r7()
    o1.r3()
    p1.r3()
    attend_b(0, (lambda i: (1 - zh, (x + 1 + 2 * i) % NX), 2))
    o.r8()
    w0.w4()
    o1.r4()
    p.r8()
    attend_b(0, (lambda i: (i, (x + 2) % NX), 2))

    size = GROUP // CHUNKS
    gsend, gshare = [], []
    for r in range(CHUNKS):
        rows = pl.ds(r * size, size)
        gat[c, rows] = gated(rows)
        gsend.append([same(gat.at[c, rows], line(k)) for k in range(1, 4)])
        gshare.append([same(gat.at[c, rows], (u, sib))])
    p1.r4()
    for r in range(CHUNKS):
        rows = pl.ds(r * size, size)
        for k in range(1, 4):
            got([gsend[r][k - 1]])
            gshare[r].append(same(gat.at[zls[4 - k] * 2 + core, rows], (u, sib)))
        if r == 0:
            o1.r5()
    w1.w1()
    p1.r5()
    for r in range(CHUNKS):
        got(gshare[r])

        @pl.loop(0, size // BLOCK)
        def _(t):
            first_row = r * size + t * BLOCK
            rows = pl.ds(pl.multiple_of(first_row, BLOCK), BLOCK)
            part = pl.ds(pl.multiple_of(r * (size // OWN) + t * 2, 2), 2)
            g = jnp.concatenate([gat[h, rows] for h in range(NC)], axis=1)
            term = jnp.dot(g, wout[0].reshape(D, D), preferred_element_type=jnp.float32)
            new = (xg[part].reshape(BLOCK, D).astype(jnp.float32) + term).astype(jnp.bfloat16)
            x1[rows, :] = new
            project(1, rows, new)

    w1.w2()
    o1.r6()
    o1.r7()
    p1.r6()
    p1.r7()
    attend_a(1, list(range(NY)))
    w1.w3()
    attend_b(1, (lambda i: (i % 2, (x + 3 + i // 2) % NX), 6))
    w1.w4()
    o1.r8()
    p1.r8()
    attend_b(1, (lambda i: (i, (x + 2) % NX), 2))
    gown[...] = gated(slice(None))
    back = []
    for k in range(1, NC):
        to = (c + k) % NC
        rows = pl.ds(pl.multiple_of(to * OWN, OWN), OWN)
        back.append(send(gown.at[rows], g1.at[c], (u, to)))
    mine = pl.ds(pl.multiple_of(c * OWN, OWN), OWN)
    g1[c] = gown[mine, :]
    got(back)
    g = jnp.concatenate([g1[h] for h in range(NC)], axis=1)
    term = jnp.dot(g, wout[1].reshape(D, D), preferred_element_type=jnp.float32)
    out_ref[...] = (x1[mine, :].astype(jnp.float32) + term).astype(jnp.bfloat16)
    for copy in sent:
        copy.wait_send()


def body(rows, weight_in, weight_out, cache, block_user, block_offset, length, count):
    bf16 = jnp.bfloat16
    hbm, smem = pl.BlockSpec(memory_space=pl.ANY), pl.BlockSpec(memory_space=pltpu.SMEM)
    return pl.pallas_call(
        kernel,
        out_shape=jax.ShapeDtypeStruct((OWN, D), bf16),
        in_specs=[hbm] * 4 + [smem] * 4,
        out_specs=pl.BlockSpec(memory_space=pltpu.VMEM),
        scratch_shapes=[
            pltpu.VMEM((2, NZ, NY, NX, 2, ROWS_A, DH), bf16),
            pltpu.VMEM((2, NZ, NX, NY, 2, ROWS_B, DH), bf16),
            pltpu.VMEM((NZ, NY, NX, ROWS_A, DH), bf16),
            pltpu.VMEM((NZ, NX, NY, ROWS_B, DH), bf16),
            pltpu.VMEM((NC, OWN, D), bf16),
            pltpu.VMEM((GROUP, D), bf16),
            pltpu.VMEM((2, D, 4 * DH), bf16),
            pltpu.VMEM((2, NC, DH, D), bf16),
            pltpu.VMEM((GROUP, 2 * DH), bf16),
            pltpu.VMEM((GROUP, DH), bf16),
            pltpu.VMEM((GROUP, DH), jnp.float32),
            pltpu.VMEM((NC, GROUP, DH), bf16),
            pltpu.VMEM((GROUP, DH), bf16),
            pltpu.VMEM((NC, OWN, DH), bf16),
            pltpu.SemaphoreType.DMA((MESSAGES,)),
            pltpu.SemaphoreType.DMA((MESSAGES,)),
            pltpu.SemaphoreType.DMA((9,)),
        ],
        compiler_params=pltpu.CompilerParams(
            collective_id=0, has_side_effects=True, vmem_limit_bytes=48 * 1024 * 1024
        ),
        cost_estimate=pl.CostEstimate(
            flops=12_000_000_000, bytes_accessed=4_000_000, transcendentals=9_000_000
        ),
    )(
        rows,
        weight_in.reshape(2, D, 4 * DH),
        weight_out.reshape(2, DH, D),
        cache.reshape(2, 2, BLOCK, DH),
        block_user,
        block_offset,
        length,
        count,
    )


def solution(mesh):
    placed = (
        P(("users", "cand"), None),
        P(None, None, "cand", None),
        P(None, "cand", None, None),
        P(None, None, "users", "cand", None),
        P(),
        P(),
        P(),
        P(),
    )
    return jax.shard_map(
        body, mesh=mesh, in_specs=placed, out_specs=P(("users", "cand"), None), check_vma=False
    )
```

time: 571 us -> 121 us (0.21)
  waiting for transfers between devices: 470 us -> 0 us
  Pallas kernels: 0 us -> 113 us
  matrix products: 64.3 us -> 0 us
  between operations: 13.6 us -> 0.02 us
  other arithmetic: 11.6 us -> 0 us
    all_gather x4 -> x0, waiting for transfers between devices: 397 us -> none  [the longest x2 315 us: body(): lax.all_gather(history_cache[layer_index], 'users', axis=1, tiled=True)]
    pallas_call x0 -> x1, Pallas kernels: none -> 113 us  [body(): pl.pallas_call(kernel, out_shape=jax.ShapeDtypeStruct((OWN, D), bf16), in...]
    reduce_scatter x2 -> x0, waiting for transfers between devices: 71.7 us -> none  [body(): lax.psum_scatter(partial_out.astype(jnp.bfloat16), 'cand', scatter_dimens...]
    dot_general x36 -> x0, matrix products: 64.3 us -> none  [the longest x32 56.5 us: block_term(): jnp.einsum('hrn,nhd->rhd', weights, key_value[1], preferred_element_type=...]
    unnamed x14 -> x17, local copies, waits for them, and re-layouts: 0.27 us -> 7.72 us
  transfers between devices with their start and end apart: 6 -> 0, of which waited for: 6 -> 0; matrix products, arithmetic and copies ran while one was open for 1% -> 0% of each run, Pallas kernels for 0% -> 0%
where the time goes in v1:
time: 121 us
  Pallas kernels  113 us (93%)
  local copies, waits for them, and re-layouts  7.72 us (6%)
    pallas_call x1, Pallas kernels, body(): pl.pallas_call(kernel, out_shape=jax.ShapeDtypeStruct((OWN, D), bf16), in...  113 us
    unnamed x17, local copies, waits for them, and re-layouts  7.72 us

profile of v1, /device:TPU:1, one launch (start us, length us, event | category | flops | bytes accessed | tf_op | source)
XLA Modules:
  0.0 120.7 jit_solution(2649019165702950701)
XLA Ops:
  0.0 0.0 copy-start
  0.0 1.6 %copy-done = bf16[2,1024,1,512]{3,1,2,0:T(8,128)(2,1)S(1)} copy-done((bf16[2,1024,1,512]{3,1,2,0:T(8,128)(2,1)S(1)}, bf16[2,1024,1,512]{3,1,2,0:T(8,128)(2,1)}, u32[]{:S(2)}) %copy-start) | copy-done | bytes 2097176
  1.6 0.0 copy-start.1
  1.6 1.0 copy-done.1
  2.6 0.0 copy-start.2
  2.6 0.9 copy-done.2
  3.5 0.0 copy-start.3
  3.5 0.9 copy-done.3
  4.4 0.0 copy-start.4
  4.4 0.7 copy-done.4
  5.1 0.0 copy-start.5
  5.1 0.7 copy-done.5
  5.8 0.0 copy-start.6
  5.8 0.7 copy-done.6
  6.4 0.0 copy-start.7
  6.4 0.7 copy-done.7
  7.1 113.0 %shard_map.82 = bf16[64,1024]{1,0:T(8,128)(2,1)S(1)} custom-call(bf16[64,1024]{1,0:T(8,128)(2,1)S(1)} %copy-done.2, bf16[2,1024,512]{2,1,0:T(8,128)(2,1)S(1)} %bitcast.3, bf16[2,128,1024]{2,1,0:T(8,128)(2,1)S(1)} %bitcast.4, bf16[2,2,128,128]{3,2,1,0:T(8,128)(2,1)S(1)} %bitcast.5, s32[64]{0:T(128)S(1)} %copy-done.4, s32[64]{0:T(128)S(1)} %copy-done.5, ...), custom_call_target="tpu_custom_call" | custom-call | flops 12000000000 | bytes 4000000 | tf_op jit(solution)/shard_map/pallas_call | solution.py:396
  120.1 0.7 copy.10
Async XLA Ops:
  0.0 1.6 %copy-start = (bf16[2,1024,1,512]{3,1,2,0:T(8,128)(2,1)S(1)}, bf16[2,1024,1,512]{3,1,2,0:T(8,128)(2,1)}, u32[]{:S(2)}) copy-start(bf16[2,1024,1,512]{3,1,2,0:T(8,128)(2,1)} %param.9) | copy-start | bytes 6291460
  1.6 1.0 copy-start.1
  2.6 0.9 copy-start.2
  3.5 0.9 copy-start.3
  4.4 0.7 copy-start.4
  5.1 0.7 copy-start.5
  5.8 0.7 copy-start.6
  6.4 0.7 copy-start.7

commit v2 on v1

--- a/solution.py
+++ b/solution.py
@@ -14,7 +14,7 @@
 GROUP = OWN * NC
 HIDE = -1e30
 CHUNKS = 2
-MESSAGES = 200
+MESSAGES = 208
 SCALE = 1.0 / math.sqrt(DH)
 
 
@@ -100,106 +100,119 @@
         def b(self, xx, *rest):
             return kvb.at[(self.l, self.z, xx) + rest]
 
-        def r0(self):
+        def a0(self):
             s = self.a(y, x)
             self.ax = [same(s, right), same(s, left)]
-            s = self.b(x, y)
-            self.by = [same(s, up), same(s, down)]
-
-        def r1(self):
+
+        def a1(self):
             got(self.ax)
             self.ax = [same(self.a(y, xs[3], 0), right), same(self.a(y, xs[1], 1), left)]
-            got(self.by)
-            self.by = [same(self.b(x, ys[7]), up), same(self.b(x, ys[1]), down)]
-
-        def r2(self):
+
+        def a2(self):
             got(self.ax)
             s = self.a(y)
             self.ay = [same(s, up), same(s, down)]
-            got(self.by)
-            self.by = [same(self.b(x, ys[6]), up), same(self.b(x, ys[2]), down)]
-
-        def r3(self):
-            got(self.by)
-            self.by = [same(self.b(x, ys[5], 0), up), same(self.b(x, ys[3], 1), down)]
+
+        def a3(self):
             got(self.ay)
             self.ay = [same(self.a(ys[7]), up), same(self.a(ys[1]), down)]
 
-        def r4(self):
-            got(self.by)
-            s = self.b(x)
-            self.bx = [same(s, right), same(s, left)]
+        def a4(self):
             got(self.ay)
             self.ay = [same(self.a(ys[6]), up), same(self.a(ys[2]), down)]
 
-        def r5(self):
+        def a5(self):
             got(self.ay)
             self.ay = [
                 same(self.a(ys[5], pl.ds(0, 2)), up),
                 same(self.a(ys[3], pl.ds(2, 2)), down),
             ]
 
-        def r6(self):
+        def a6(self):
             got(self.ay)
 
-        def r7(self):
+        def row(self, *at_y):
+            for yy in at_y:
+                s = self.b(x, yy)
+                self.bx += [same(s, right), same(s, left)]
+
+        def b0(self):
+            s = self.b(x, y)
+            self.by, self.bx = [same(s, up), same(s, down)], []
+            self.row(y)
+
+        def b1(self):
+            got(self.by)
+            self.by = [same(self.b(x, ys[7]), up), same(self.b(x, ys[1]), down)]
+            self.row(ys[7], ys[1])
+
+        def b2(self):
+            got(self.by)
+            self.by = [same(self.b(x, ys[6]), up), same(self.b(x, ys[2]), down)]
+            self.row(ys[6], ys[2])
+
+        def b3(self):
+            got(self.by)
+            self.by = [same(self.b(x, ys[5], 0), up), same(self.b(x, ys[3], 1), down)]
+            self.row(ys[5], ys[3])
+
+        def b4(self):
+            got(self.by)
+            self.row(ys[4])
+
+        def b5(self):
             got(self.bx)
             self.bx = [
                 same(self.b(xs[3], pl.ds(0, 4)), right),
                 same(self.b(xs[1], pl.ds(4, 4)), left),
             ]
 
-        def r8(self):
+        def b6(self):
             got(self.bx)
 
-    def scores(rows, k, m, v):
+    def scores(k, m, v):
         s = lax.dot_general(
-            qp[rows, :], jnp.concatenate([k, m], axis=1), (((1,), (1,)), ((), ())),
+            qp[...], jnp.concatenate([k, m], axis=1), (((1,), (1,)), ((), ())),
             preferred_element_type=jnp.float32,
         )
-        w = half_silu(jnp.maximum(s * (0.5 * SCALE), -100.0)).astype(jnp.bfloat16)
-        acc[rows, :] += jnp.dot(w, v, preferred_element_type=jnp.float32)
-
-    def attend_a(l, offsets):
-        low, step = offsets[0], (offsets[1] - offsets[0]) if len(offsets) > 1 else 1
-
-        @pl.loop(0, 2 * len(offsets))
+        w = half_silu(s.astype(jnp.bfloat16))
+        acc[...] += jnp.dot(w, v, preferred_element_type=jnp.float32)
+
+    def attend_a(l, low, number):
+        @pl.loop(low, low + number)
         def _(i):
-            yy = (y + low + (i // 2) * step) % NY
-            rows = pl.ds(pl.multiple_of((i % 2) * 256, 256), 256)
             n = NZ * NX * ROWS_A
+
+            def both(ref, *rest):
+                return jnp.concatenate([
+                    ref[(slice(None), yy, slice(None)) + rest].reshape(n, DH)
+                    for yy in ((y + NY - i) % NY, (y + 1 + i) % NY)
+                ])
+
+            scores(both(kva.at[l], 0), both(ma), both(kva.at[l], 1))
+
+    def attend_b(l, low, number):
+        @pl.loop(low, low + number)
+        def _(i):
+            xx = (x + i) % NX
+            n = NZ * NY * ROWS_B
             scores(
-                rows,
-                kva[l, :, yy, :, 0].reshape(n, DH),
-                ma[:, yy].reshape(n, DH),
-                kva[l, :, yy, :, 1].reshape(n, DH),
-            )
-
-    def attend_b(l, chunks):
-        where, number = chunks
-
-        @pl.loop(0, 2 * number)
-        def _(i):
-            zz, xx = where(i // 2)
-            rows = pl.ds(pl.multiple_of((i % 2) * 256, 256), 256)
-            n = NY * ROWS_B
-            scores(
-                rows,
-                kvb[l, zz, xx, :, 0].reshape(n, DH),
-                mb[zz, xx].reshape(n, DH),
-                kvb[l, zz, xx, :, 1].reshape(n, DH),
+                kvb[l, :, xx, :, 0].reshape(n, DH),
+                mb[:, xx].reshape(n, DH),
+                kvb[l, :, xx, :, 1].reshape(n, DH),
             )
 
     def project(l, rows, value):
         mixed = jnp.dot(value, win[l], preferred_element_type=jnp.float32)
-        p = half_silu(0.5 * mixed).astype(jnp.bfloat16)
-        q = p[:, 2 * DH:3 * DH]
+        p = half_silu(0.5 * mixed)
+        q = (p[:, 2 * DH:3 * DH] * (0.5 * SCALE)).astype(jnp.bfloat16)
+        p = p.astype(jnp.bfloat16)
         gate[rows, :] = p[:, :DH]
         qp[rows, pl.ds(0, DH)] = q
         own = jnp.sum(
             q.astype(jnp.float32) * p[:, 3 * DH:].astype(jnp.float32), axis=1, keepdims=True
         )
-        own = half_silu(own * (0.5 * SCALE)).astype(jnp.bfloat16).astype(jnp.float32)
+        own = half_silu(own).astype(jnp.bfloat16).astype(jnp.float32)
         acc[rows, :] = own * p[:, DH:2 * DH].astype(jnp.float32)
 
     def gated(rows):
@@ -239,16 +252,15 @@
 
     for copy in first:
         copy.wait()
+    def cross(l):
+        return [same(kva.at[l, zh, y, x], over), same(kvb.at[l, zh, x, y], over)]
+
+    across = [cross(0)]
+    (o, p), (o1, p1) = [[Chain(l, zh), Chain(l, 1 - zh)] for l in range(2)]
+    o.b0()
+    o.a0()
     xsend = [same(xg.at[c], line(k)) for k in range(1, 4)]
     xshare = [same(xg.at[c], (u, sib))]
-    across = []
-    for l in range(2):
-        across.append([same(kva.at[l, zh, y, x], over), same(kvb.at[l, zh, x, y], over)])
-        if l == 0:
-            chains = [[Chain(i, zh), Chain(i, 1 - zh)] for i in range(2)]
-            o, p = chains[0]
-            o.r0()
-    o1, p1 = chains[1]
     w0, w1 = Weights(0), Weights(1)
 
     lane = lax.broadcasted_iota(jnp.int32, (BLOCK, BLOCK), 1)
@@ -263,8 +275,6 @@
         hot = jnp.where(lane == code, 1.0, 0.0).astype(jnp.bfloat16)
         ma[bz, by, bx] = hot[:ROWS_A]
         mb[bz, bx, by] = hot[ROWS_A:]
-
-    o.r1()
 
     @pl.loop(0, GROUP // BLOCK)
     def _(t):
@@ -277,19 +287,30 @@
         hide = jnp.where((lane == cu) | (lane > USERS), 0.0, HIDE)
         qp[pl.ds(pl.multiple_of(t * BLOCK, BLOCK), BLOCK), pl.ds(DH, DH)] = hide.astype(jnp.bfloat16)
 
+    o.b1()
+    o.a1()
+    o.b2()
     got(across[0])
-    p.r0()
-    o.r2()
-    p.r1()
-    o.r3()
+    p.b0()
+    p.a0()
+    o.a2()
+    o.b3()
+    p.b1()
+    p.a1()
+    o.a3()
+    o.b4()
+    p.b2()
+    p.a2()
+    o.a4()
+    o.b5()
     for k in range(1, 4):
         got([xsend[k - 1]])
         xshare.append(same(xg.at[zls[4 - k] * 2 + core], (u, sib)))
+    across.append(cross(1))
     for copy in second:
         copy.wait()
     w0.w1()
-    p.r2()
-    o.r4()
+    p.b3()
     for copy in third:
         copy.wait()
     got(xshare)
@@ -300,37 +321,39 @@
         rows = pl.ds(pl.multiple_of(t * BLOCK, BLOCK), BLOCK)
         project(0, rows, xg[part].reshape(BLOCK, D))
 
-    p.r3()
+    p.a3()
+    attend_a(0, 0, 1)
+    o.a5()
+    o.b6()
+    p.b4()
+    attend_b(0, 0, 1)
+    o1.b0()
+    got(across[1])
+    p1.b0()
+    o1.a0()
+    p1.a0()
     w0.w2()
-    o.r5()
-    p.r4()
-    attend_a(0, [-1 + NY, NY, NY + 1])
-    got(across[1])
-    o1.r0()
-    p1.r0()
+    p.a4()
+    attend_a(0, 1, 1)
+    p.b5()
+    attend_b(0, 1, 1)
+    o.a6()
+    attend_b(0, 3, 1)
+    o1.b1()
+    o1.a1()
+    p1.b1()
+    p1.a1()
+    p.a5()
     w0.w3()
-    p.r5()
-    o.r6()
-    attend_a(0, [2, 6])
-    o1.r1()
-    p1.r1()
-    p.r6()
-    attend_b(0, (lambda i: (i, x), 2))
-    o.r7()
-    o1.r2()
-    p1.r2()
-    attend_a(0, [3, 4, 5])
-    attend_b(0, (lambda i: (zh, (x + 1 + 2 * i) % NX), 2))
-    p.r7()
-    o1.r3()
-    p1.r3()
-    attend_b(0, (lambda i: (1 - zh, (x + 1 + 2 * i) % NX), 2))
-    o.r8()
-    w0.w4()
-    o1.r4()
-    p.r8()
-    attend_b(0, (lambda i: (i, (x + 2) % NX), 2))
-
+    attend_a(0, 2, 1)
+    o1.b2()
+    p.b6()
+    p1.b2()
+    attend_b(0, 2, 1)
+    p.a6()
+    attend_a(0, 3, 1)
+    o1.b3()
+    o1.a2()
     size = GROUP // CHUNKS
     gsend, gshare = [], []
     for r in range(CHUNKS):
@@ -338,17 +361,13 @@
         gat[c, rows] = gated(rows)
         gsend.append([same(gat.at[c, rows], line(k)) for k in range(1, 4)])
         gshare.append([same(gat.at[c, rows], (u, sib))])
-    p1.r4()
-    for r in range(CHUNKS):
+    def pass_on(r):
         rows = pl.ds(r * size, size)
         for k in range(1, 4):
             got([gsend[r][k - 1]])
             gshare[r].append(same(gat.at[zls[4 - k] * 2 + core, rows], (u, sib)))
-        if r == 0:
-            o1.r5()
-    w1.w1()
-    p1.r5()
-    for r in range(CHUNKS):
+
+    def next_layer(r):
         got(gshare[r])
 
         @pl.loop(0, size // BLOCK)
@@ -362,27 +381,48 @@
             x1[rows, :] = new
             project(1, rows, new)
 
+    p1.b3()
+    p1.a2()
+    o1.b4()
+    o1.a3()
+    p1.b4()
+    pass_on(0)
+    w0.w4()
+    next_layer(0)
+    p1.a3()
+    o1.a4()
+    pass_on(1)
+    w1.w1()
+    o1.b5()
+    p1.b5()
+    next_layer(1)
+    p1.a4()
+    attend_a(1, 0, 1)
+    attend_a(1, 1, 1)
+    o1.a5()
+    attend_b(1, 0, 1)
+    o1.b6()
     w1.w2()
-    o1.r6()
-    o1.r7()
-    p1.r6()
-    p1.r7()
-    attend_a(1, list(range(NY)))
-    w1.w3()
-    attend_b(1, (lambda i: (i % 2, (x + 3 + i // 2) % NX), 6))
-    w1.w4()
-    o1.r8()
-    p1.r8()
-    attend_b(1, (lambda i: (i, (x + 2) % NX), 2))
+    attend_b(1, 1, 1)
+    attend_b(1, 3, 1)
+    p1.a5()
+    attend_a(1, 2, 1)
+    o1.a6()
+    p1.b6()
+    attend_b(1, 2, 1)
+    p1.a6()
+    attend_a(1, 3, 1)
     gown[...] = gated(slice(None))
     back = []
     for k in range(1, NC):
         to = (c + k) % NC
         rows = pl.ds(pl.multiple_of(to * OWN, OWN), OWN)
         back.append(send(gown.at[rows], g1.at[c], (u, to)))
+    w1.w3()
     mine = pl.ds(pl.multiple_of(c * OWN, OWN), OWN)
     g1[c] = gown[mine, :]
     got(back)
+    w1.w4()
     g = jnp.concatenate([g1[h] for h in range(NC)], axis=1)
     term = jnp.dot(g, wout[1].reshape(D, D), preferred_element_type=jnp.float32)
     out_ref[...] = (x1[mine, :].astype(jnp.float32) + term).astype(jnp.bfloat16)
@@ -418,7 +458,7 @@
             pltpu.SemaphoreType.DMA((9,)),
         ],
         compiler_params=pltpu.CompilerParams(
-            collective_id=0, has_side_effects=True, vmem_limit_bytes=48 * 1024 * 1024
+            collective_id=0, has_side_effects=True, vmem_limit_bytes=60 * 1024 * 1024
         ),
         cost_estimate=pl.CostEstimate(
             flops=12_000_000_000, bytes_accessed=4_000_000, transcendentals=9_000_000

time: 121 us -> 90.3 us (0.75)
  Pallas kernels: 113 us -> 88.6 us
  local copies, waits for them, and re-layouts: 7.72 us -> 1.57 us
    pallas_call x1, Pallas kernels: 113 us -> 88.6 us  [body(): pl.pallas_call(kernel, out_shape=jax.ShapeDtypeStruct((OWN, D), bf16), in...]
    unnamed x17 -> x1, local copies, waits for them, and re-layouts: 7.72 us -> 1.57 us
where the time goes in v2:
time: 90.3 us; the launch traced here: 90.2 us
  Pallas kernels  88.6 us (98%)
  local copies, waits for them, and re-layouts  1.57 us (2%)
    pallas_call x1, Pallas kernels, body(): pl.pallas_call(kernel, out_shape=jax.ShapeDtypeStruct((OWN, D), bf16), in...  88.6 us

profile of v2, /device:TPU:1, one launch (start us, length us, event | category | flops | bytes accessed | tf_op | source)
XLA Modules:
  0.0 90.2 jit_solution(11208546611044236130)
XLA Ops:
  0.0 88.6 %shard_map.82 = bf16[64,1024]{1,0:T(8,128)(2,1)} custom-call(bf16[64,1024]{1,0:T(8,128)(2,1)} %x_ref.1, bf16[2,1024,512]{2,1,0:T(8,128)(2,1)} %bitcast.3, bf16[2,128,1024]{2,1,0:T(8,128)(2,1)} %bitcast.4, bf16[2,2,128,128]{3,2,1,0:T(8,128)(2,1)} %bitcast.5, s32[64]{0:T(128)} %user_ref.1, s32[64]{0:T(128)} %place_ref.1, s32[16]{0:T(128)} %length_ref.1, ...), custom_call_target="tpu_custom_call" | custom-call | flops 12000000000 | bytes 4000000 | tf_op jit(solution)/shard_map/pallas_call | solution.py:436
  88.6 1.6 %copy.10 = bf16[64,1024]{1,0:T(8,128)(2,1)} copy(bf16[64,1024]{1,0:T(8,128)(2,1)} %shard_map.82) | data formatting | bytes 262144

commit v3 on v2

--- a/solution.py
+++ b/solution.py
@@ -14,7 +14,7 @@
 GROUP = OWN * NC
 HIDE = -1e30
 CHUNKS = 2
-MESSAGES = 208
+ARRIVALS, DEPARTURES = 80, 11
 SCALE = 1.0 / math.sqrt(DH)
 
 
@@ -23,9 +23,9 @@
 
 
 def kernel(
-    x_ref, win_ref, wout_ref, hist_ref, user_ref, place_ref, length_ref, count_ref, out_ref,
+    x_ref, win_ref, wout_ref, hist_ref, user_in, place_in, length_in, count_in, out_ref,
     kva, kvb, ma, mb, xg, x1, win, wout, qp, gate, acc, gat, gown, g1,
-    send_sem, recv_sem, local_sem,
+    user_ref, place_ref, length_ref, count_ref, send_sem, recv_sem, local_sem,
 ):
     u, c = lax.axis_index("users"), lax.axis_index("cand")
     y, zh, x = u // 8, (u // 4) % 2, u % 4
@@ -61,6 +61,12 @@
     for l in range(2):
         first.append(fetch(hist_ref.at[l, :, pl.ds(0, ROWS_A)], kva.at[l, zh, y, x]))
         first.append(fetch(hist_ref.at[l, :, pl.ds(ROWS_A, ROWS_B)], kvb.at[l, zh, x, y]))
+    small = [
+        fetch(src, dst)
+        for src, dst in (
+            (user_in, user_ref), (place_in, place_ref), (length_in, length_ref), (count_in, count_ref)
+        )
+    ]
     second = [fetch(wout_ref.at[l], wout.at[l, c]) for l in range(2)]
     third = [fetch(win_ref.at[l], win.at[l]) for l in range(2)]
 
@@ -71,24 +77,28 @@
         pl.semaphore_signal(barrier, inc=1, device_id=friend, device_id_type=pl.DeviceIdType.MESH)
     pl.semaphore_wait(barrier, len(friends))
 
-    sent = []
-
-    def send(src, dst, to):
-        n = len(sent)
-        copy = pltpu.make_async_remote_copy(
-            src_ref=src, dst_ref=dst, send_sem=send_sem.at[n], recv_sem=recv_sem.at[n],
-            device_id=to, device_id_type=pl.DeviceIdType.MESH,
-        )
-        copy.start()
-        sent.append(copy)
-        return copy
-
-    def same(ref, to):
-        return send(ref, ref, to)
-
-    def got(copies):
-        for copy in copies:
-            copy.wait_recv()
+    AY, AX, BY, BH, BX, CA, CB, XS, WS, GS, HS = range(DEPARTURES)
+    arrivals = []
+
+    class Batch:
+        def __init__(self, size):
+            self.sem, self.size = recv_sem.at[len(arrivals)], size
+            arrivals.append(self)
+
+        def send(self, kind, src, dst, to):
+            pltpu.make_async_remote_copy(
+                src_ref=src, dst_ref=dst, send_sem=send_sem.at[kind], recv_sem=self.sem,
+                device_id=to, device_id_type=pl.DeviceIdType.MESH,
+            ).start()
+            return self
+
+        def same(self, kind, *pairs):
+            for ref, to in pairs:
+                self.send(kind, ref, ref, to)
+            return self
+
+        def got(self):
+            pltpu.make_async_copy(self.size, self.size, self.sem).wait()
 
     class Chain:
         def __init__(self, l, z):
@@ -102,73 +112,84 @@
 
         def a0(self):
             s = self.a(y, x)
-            self.ax = [same(s, right), same(s, left)]
+            self.ax = Batch(kva.at[0, 0, 0, pl.ds(0, 2)]).same(AX, (s, right), (s, left))
 
         def a1(self):
-            got(self.ax)
-            self.ax = [same(self.a(y, xs[3], 0), right), same(self.a(y, xs[1], 1), left)]
+            self.ax.got()
+            self.ax = Batch(kva.at[0, 0, 0, 0]).same(
+                AX, (self.a(y, xs[3], 0), right), (self.a(y, xs[1], 1), left)
+            )
+
+        def go_y(self, one, other):
+            self.ay = Batch(kva.at[0, 0, pl.ds(0, 2)]).same(
+                AY, (self.a(one), up), (self.a(other), down)
+            )
 
         def a2(self):
-            got(self.ax)
-            s = self.a(y)
-            self.ay = [same(s, up), same(s, down)]
+            self.ax.got()
+            self.go_y(y, y)
 
         def a3(self):
-            got(self.ay)
-            self.ay = [same(self.a(ys[7]), up), same(self.a(ys[1]), down)]
+            self.ay.got()
+            self.go_y(ys[7], ys[1])
 
         def a4(self):
-            got(self.ay)
-            self.ay = [same(self.a(ys[6]), up), same(self.a(ys[2]), down)]
+            self.ay.got()
+            self.go_y(ys[6], ys[2])
 
         def a5(self):
-            got(self.ay)
-            self.ay = [
-                same(self.a(ys[5], pl.ds(0, 2)), up),
-                same(self.a(ys[3], pl.ds(2, 2)), down),
-            ]
+            self.ay.got()
+            self.ay = Batch(kva.at[0, 0, 0]).same(
+                AX, (self.a(ys[5], pl.ds(0, 2)), up), (self.a(ys[3], pl.ds(2, 2)), down)
+            )
 
         def a6(self):
-            got(self.ay)
+            self.ay.got()
 
         def row(self, *at_y):
             for yy in at_y:
                 s = self.b(x, yy)
-                self.bx += [same(s, right), same(s, left)]
+                self.bx.same(BX, (s, right), (s, left))
+
+        def go_b(self, one, other):
+            self.by = Batch(kvb.at[0, 0, 0, pl.ds(0, 2)]).same(
+                BY, (self.b(x, one), up), (self.b(x, other), down)
+            )
 
         def b0(self):
-            s = self.b(x, y)
-            self.by, self.bx = [same(s, up), same(s, down)], []
+            self.bx = Batch(kvb.at[0, 0, pl.ds(0, 2)])
+            self.go_b(y, y)
             self.row(y)
 
         def b1(self):
-            got(self.by)
-            self.by = [same(self.b(x, ys[7]), up), same(self.b(x, ys[1]), down)]
+            self.by.got()
+            self.go_b(ys[7], ys[1])
             self.row(ys[7], ys[1])
 
         def b2(self):
-            got(self.by)
-            self.by = [same(self.b(x, ys[6]), up), same(self.b(x, ys[2]), down)]
+            self.by.got()
+            self.go_b(ys[6], ys[2])
             self.row(ys[6], ys[2])
 
         def b3(self):
-            got(self.by)
-            self.by = [same(self.b(x, ys[5], 0), up), same(self.b(x, ys[3], 1), down)]
+            self.by.got()
+            self.by = Batch(kvb.at[0, 0, 0, 0]).same(
+                BH, (self.b(x, ys[5], 0), up), (self.b(x, ys[3], 1), down)
+            )
             self.row(ys[5], ys[3])
 
         def b4(self):
-            got(self.by)
+            self.by.got()
             self.row(ys[4])
 
         def b5(self):
-            got(self.bx)
-            self.bx = [
-                same(self.b(xs[3], pl.ds(0, 4)), right),
-                same(self.b(xs[1], pl.ds(4, 4)), left),
-            ]
+            self.bx.got()
+            self.bx = Batch(kvb.at[0, 0, 0]).same(
+                BX, (self.b(xs[3], pl.ds(0, 4)), right), (self.b(xs[1], pl.ds(4, 4)), left)
+            )
 
         def b6(self):
-            got(self.bx)
+            self.bx.got()
 
     def scores(k, m, v):
         s = lax.dot_general(
@@ -232,39 +253,49 @@
 
         def w1(self):
             s = wout.at[self.l, c]
-            self.z = [same(s, ring_up), same(s, ring_down)]
-            self.s = [same(s, (u, sib))]
+            self.z = Batch(wout.at[0, pl.ds(0, 2)]).same(WS, (s, ring_up), (s, ring_down))
+            self.s = Batch(wout.at[0, pl.ds(0, 4)]).same(WS, (s, (u, sib)))
 
         def w2(self):
-            got(self.z)
+            self.z.got()
             below, above = wout.at[self.l, self.slot(3)], wout.at[self.l, self.slot(1)]
-            self.z = [
-                same(below.at[pl.ds(0, 64)], ring_up), same(above.at[pl.ds(64, 64)], ring_down)
-            ]
-            self.s += [same(below, (u, sib)), same(above, (u, sib))]
+            self.z = Batch(wout.at[0, 0]).same(
+                WS, (below.at[pl.ds(0, 64)], ring_up), (above.at[pl.ds(64, 64)], ring_down)
+            )
+            self.s.same(WS, (below, (u, sib)), (above, (u, sib)))
 
         def w3(self):
-            got(self.z)
-            self.s += [same(wout.at[self.l, self.slot(2)], (u, sib))]
+            self.z.got()
+            self.s.same(WS, (wout.at[self.l, self.slot(2)], (u, sib)))
 
         def w4(self):
-            got(self.s)
+            self.s.got()
 
     for copy in first:
         copy.wait()
     def cross(l):
-        return [same(kva.at[l, zh, y, x], over), same(kvb.at[l, zh, x, y], over)]
+        return [
+            Batch(kva.at[0, 0, 0, 0]).same(CA, (kva.at[l, zh, y, x], over)),
+            Batch(kvb.at[0, 0, 0, 0]).same(CB, (kvb.at[l, zh, x, y], over)),
+        ]
+
+    def crossed(l):
+        for batch in across[l]:
+            batch.got()
 
     across = [cross(0)]
     (o, p), (o1, p1) = [[Chain(l, zh), Chain(l, 1 - zh)] for l in range(2)]
     o.b0()
     o.a0()
-    xsend = [same(xg.at[c], line(k)) for k in range(1, 4)]
-    xshare = [same(xg.at[c], (u, sib))]
     w0, w1 = Weights(0), Weights(1)
 
     lane = lax.broadcasted_iota(jnp.int32, (BLOCK, BLOCK), 1)
     sub = lax.broadcasted_iota(jnp.int32, (BLOCK, BLOCK), 0)
+
+    xsend = [Batch(xg.at[0]).same(XS, (xg.at[c], line(k))) for k in range(1, 4)]
+    xshare = Batch(xg.at[pl.ds(0, 4)]).same(XS, (xg.at[c], (u, sib)))
+    for copy in small:
+        copy.wait()
 
     @pl.loop(0, NX * NY * NZ)
     def _(b):
@@ -290,30 +321,27 @@
     o.b1()
     o.a1()
     o.b2()
-    got(across[0])
+    crossed(0)
     p.b0()
     p.a0()
     o.a2()
-    o.b3()
     p.b1()
     p.a1()
+    o.b3()
     o.a3()
+    p.b2()
     o.b4()
-    p.b2()
     p.a2()
-    o.a4()
-    o.b5()
     for k in range(1, 4):
-        got([xsend[k - 1]])
-        xshare.append(same(xg.at[zls[4 - k] * 2 + core], (u, sib)))
+        xsend[k - 1].got()
+        xshare.same(XS, (xg.at[zls[4 - k] * 2 + core], (u, sib)))
     across.append(cross(1))
     for copy in second:
         copy.wait()
     w0.w1()
-    p.b3()
     for copy in third:
         copy.wait()
-    got(xshare)
+    xshare.got()
 
     @pl.loop(0, 4)
     def _(t):
@@ -321,54 +349,66 @@
         rows = pl.ds(pl.multiple_of(t * BLOCK, BLOCK), BLOCK)
         project(0, rows, xg[part].reshape(BLOCK, D))
 
+    p.b3()
+    o.a4()
+    o.b5()
     p.a3()
     attend_a(0, 0, 1)
-    o.a5()
-    o.b6()
     p.b4()
     attend_b(0, 0, 1)
     o1.b0()
-    got(across[1])
+    crossed(1)
     p1.b0()
     o1.a0()
     p1.a0()
     w0.w2()
+    o.a5()
     p.a4()
     attend_a(0, 1, 1)
+    o.b6()
+    o1.b1()
     p.b5()
     attend_b(0, 1, 1)
+    p1.b1()
+    w0.w3()
+    w1.w1()
+    attend_b(0, 3, 1)
     o.a6()
-    attend_b(0, 3, 1)
-    o1.b1()
     o1.a1()
-    p1.b1()
     p1.a1()
     p.a5()
-    w0.w3()
     attend_a(0, 2, 1)
     o1.b2()
-    p.b6()
     p1.b2()
-    attend_b(0, 2, 1)
     p.a6()
     attend_a(0, 3, 1)
     o1.b3()
-    o1.a2()
+    p1.b3()
+    p.b6()
+    attend_b(0, 2, 1)
     size = GROUP // CHUNKS
+    halves = [pl.ds(r * size, size) for r in range(CHUNKS)]
     gsend, gshare = [], []
-    for r in range(CHUNKS):
-        rows = pl.ds(r * size, size)
-        gat[c, rows] = gated(rows)
-        gsend.append([same(gat.at[c, rows], line(k)) for k in range(1, 4)])
-        gshare.append([same(gat.at[c, rows], (u, sib))])
+
+    def spread(r):
+        own = gat.at[c, halves[r]]
+        one = gat.at[0, pl.ds(0, size)]
+        gsend.append([Batch(one).same(GS, (own, line(k))) for k in range(1, 4)])
+        gshare.append(
+            Batch(gat.at[pl.ds(0, 4), pl.ds(0, size)]).same(GS, (own, (u, sib)))
+        )
+
+    gat[c, halves[0]] = gated(halves[0])
+    spread(0)
+    gat[c, halves[1]] = gated(halves[1])
+
     def pass_on(r):
-        rows = pl.ds(r * size, size)
         for k in range(1, 4):
-            got([gsend[r][k - 1]])
-            gshare[r].append(same(gat.at[zls[4 - k] * 2 + core, rows], (u, sib)))
+            gsend[r][k - 1].got()
+            gshare[r].same(GS, (gat.at[zls[4 - k] * 2 + core, halves[r]], (u, sib)))
 
     def next_layer(r):
-        got(gshare[r])
+        gshare[r].got()
 
         @pl.loop(0, size // BLOCK)
         def _(t):
@@ -381,30 +421,31 @@
             x1[rows, :] = new
             project(1, rows, new)
 
-    p1.b3()
+    o1.b4()
+    o1.a2()
+    p1.b4()
     p1.a2()
-    o1.b4()
     o1.a3()
-    p1.b4()
     pass_on(0)
+    spread(1)
+    p1.a3()
     w0.w4()
     next_layer(0)
-    p1.a3()
     o1.a4()
+    o1.b5()
+    p1.a4()
     pass_on(1)
-    w1.w1()
-    o1.b5()
     p1.b5()
     next_layer(1)
-    p1.a4()
+    w1.w2()
     attend_a(1, 0, 1)
     attend_a(1, 1, 1)
     o1.a5()
+    o1.b6()
     attend_b(1, 0, 1)
-    o1.b6()
-    w1.w2()
     attend_b(1, 1, 1)
     attend_b(1, 3, 1)
+    w1.w3()
     p1.a5()
     attend_a(1, 2, 1)
     o1.a6()
@@ -413,30 +454,42 @@
     p1.a6()
     attend_a(1, 3, 1)
     gown[...] = gated(slice(None))
-    back = []
+    back = Batch(g1.at[pl.ds(0, NC - 1)])
     for k in range(1, NC):
         to = (c + k) % NC
         rows = pl.ds(pl.multiple_of(to * OWN, OWN), OWN)
-        back.append(send(gown.at[rows], g1.at[c], (u, to)))
-    w1.w3()
+        back.send(HS, gown.at[rows], g1.at[c], (u, to))
     mine = pl.ds(pl.multiple_of(c * OWN, OWN), OWN)
     g1[c] = gown[mine, :]
-    got(back)
+    back.got()
     w1.w4()
     g = jnp.concatenate([g1[h] for h in range(NC)], axis=1)
     term = jnp.dot(g, wout[1].reshape(D, D), preferred_element_type=jnp.float32)
     out_ref[...] = (x1[mine, :].astype(jnp.float32) + term).astype(jnp.bfloat16)
-    for copy in sent:
-        copy.wait_send()
+    everything = {
+        AY: kva.at[:, :, pl.ds(0, 6)],
+        AX: kva.at[0, 0, pl.ds(0, 7)],
+        BY: kvb.at[0, 0, pl.ds(0, 3)],
+        BH: kvb.at[0, 0, 0, pl.ds(0, 4)],
+        BX: kvb.at[:, :, pl.ds(0, 3)],
+        CA: kva.at[0, 0, 0, pl.ds(0, 2)],
+        CB: kvb.at[0, 0, 0, pl.ds(0, 2)],
+        XS: xg.at[pl.ds(0, 7)],
+        WS: wout.at[:, pl.ds(0, 7)],
+        GS: gat.at[pl.ds(0, 7)],
+        HS: g1.at[pl.ds(0, 7)],
+    }
+    for kind, size_ref in everything.items():
+        pltpu.make_async_copy(size_ref, size_ref, send_sem.at[kind]).wait()
 
 
 def body(rows, weight_in, weight_out, cache, block_user, block_offset, length, count):
     bf16 = jnp.bfloat16
-    hbm, smem = pl.BlockSpec(memory_space=pl.ANY), pl.BlockSpec(memory_space=pltpu.SMEM)
+    hbm = pl.BlockSpec(memory_space=pl.ANY)
     return pl.pallas_call(
         kernel,
         out_shape=jax.ShapeDtypeStruct((OWN, D), bf16),
-        in_specs=[hbm] * 4 + [smem] * 4,
+        in_specs=[hbm] * 8,
         out_specs=pl.BlockSpec(memory_space=pltpu.VMEM),
         scratch_shapes=[
             pltpu.VMEM((2, NZ, NY, NX, 2, ROWS_A, DH), bf16),
@@ -453,9 +506,13 @@
             pltpu.VMEM((NC, GROUP, DH), bf16),
             pltpu.VMEM((GROUP, DH), bf16),
             pltpu.VMEM((NC, OWN, DH), bf16),
-            pltpu.SemaphoreType.DMA((MESSAGES,)),
-            pltpu.SemaphoreType.DMA((MESSAGES,)),
-            pltpu.SemaphoreType.DMA((9,)),
+            pltpu.SMEM((64,), jnp.int32),
+            pltpu.SMEM((64,), jnp.int32),
+            pltpu.SMEM((16,), jnp.int32),
+            pltpu.SMEM((16,), jnp.int32),
+            pltpu.SemaphoreType.DMA((DEPARTURES,)),
+            pltpu.SemaphoreType.DMA((ARRIVALS,)),
+            pltpu.SemaphoreType.DMA((13,)),
         ],
         compiler_params=pltpu.CompilerParams(
             collective_id=0, has_side_effects=True, vmem_limit_bytes=60 * 1024 * 1024

time: 90.3 us -> 86.5 us (0.958)
  Pallas kernels: 88.6 us -> 84.8 us
    pallas_call x1, Pallas kernels: 88.6 us -> 84.8 us  [body(): pl.pallas_call(kernel, out_shape=jax.ShapeDtypeStruct((OWN, D), bf16), in...]
where the time goes in v3:
time: 86.5 us; the launch traced here: 86.4 us
  Pallas kernels  84.8 us (98%)
  local copies, waits for them, and re-layouts  1.57 us (2%)
    pallas_call x1, Pallas kernels, body(): pl.pallas_call(kernel, out_shape=jax.ShapeDtypeStruct((OWN, D), bf16), in...  84.8 us

profile of v3, /device:TPU:1, one launch (start us, length us, event | category | flops | bytes accessed | tf_op | source)
XLA Modules:
  0.0 86.4 jit_solution(11890511363485103230)
XLA Ops:
  0.0 84.8 %shard_map.82 = bf16[64,1024]{1,0:T(8,128)(2,1)} custom-call(bf16[64,1024]{1,0:T(8,128)(2,1)} %x_ref.1, bf16[2,1024,512]{2,1,0:T(8,128)(2,1)} %bitcast.3, bf16[2,128,1024]{2,1,0:T(8,128)(2,1)} %bitcast.4, bf16[2,2,128,128]{3,2,1,0:T(8,128)(2,1)} %bitcast.5, s32[64]{0:T(128)} %user_in.1, s32[64]{0:T(128)} %place_in.1, s32[16]{0:T(128)} %length_in.1, s32[16]{0:T(128)} %count_in.1), custom_call_target="tpu_custom_call" | custom-call | flops 12000000000 | bytes 4000000 | tf_op jit(solution)/shard_map/pallas_call | solution.py:489
  84.8 1.6 %copy.10 = bf16[64,1024]{1,0:T(8,128)(2,1)} copy(bf16[64,1024]{1,0:T(8,128)(2,1)} %shard_map.82) | data formatting | bytes 262144

commit v4 on v3

--- a/solution.py
+++ b/solution.py
@@ -196,7 +196,7 @@
             qp[...], jnp.concatenate([k, m], axis=1), (((1,), (1,)), ((), ())),
             preferred_element_type=jnp.float32,
         )
-        w = half_silu(s.astype(jnp.bfloat16))
+        w = half_silu(jnp.maximum(s, -100.0)).astype(jnp.bfloat16)
         acc[...] += jnp.dot(w, v, preferred_element_type=jnp.float32)
 
     def attend_a(l, low, number):

time: 86.5 us -> 87.2 us (level)
  no operation moved by 1% of the time
where the time goes in v4:
time: 87.2 us; the launch traced here: 86.3 us
  Pallas kernels  84.8 us (97%)
  local copies, waits for them, and re-layouts  1.57 us (2%)
    pallas_call x1, Pallas kernels, body(): pl.pallas_call(kernel, out_shape=jax.ShapeDtypeStruct((OWN, D), bf16), in...  84.8 us

profile of v4, /device:TPU:1, one launch (start us, length us, event | category | flops | bytes accessed | tf_op | source)
XLA Modules:
  0.0 86.3 jit_solution(207311164496423667)
XLA Ops:
  0.0 84.8 %shard_map.82 = bf16[64,1024]{1,0:T(8,128)(2,1)} custom-call(bf16[64,1024]{1,0:T(8,128)(2,1)} %x_ref.1, bf16[2,1024,512]{2,1,0:T(8,128)(2,1)} %bitcast.3, bf16[2,128,1024]{2,1,0:T(8,128)(2,1)} %bitcast.4, bf16[2,2,128,128]{3,2,1,0:T(8,128)(2,1)} %bitcast.5, s32[64]{0:T(128)} %user_in.1, s32[64]{0:T(128)} %place_in.1, s32[16]{0:T(128)} %length_in.1, s32[16]{0:T(128)} %count_in.1), custom_call_target="tpu_custom_call" | custom-call | flops 12000000000 | bytes 4000000 | tf_op jit(solution)/shard_map/pallas_call | solution.py:489
  84.8 1.6 %copy.10 = bf16[64,1024]{1,0:T(8,128)(2,1)} copy(bf16[64,1024]{1,0:T(8,128)(2,1)} %shard_map.82) | data formatting | bytes 262144
